TPU v7x, 128 devices: a whole 4x4x4 slice. The times are simulated.
128 devices in a mesh: samp: 64 (over x, y_hi, z, core), snp: 2 (over y_lo).
Axes of the slice: x: 4, y: 4 (y_hi: 2, y_lo: 2; y = y_hi * 2 + y_lo), z: 4, core: 2. Of those that a mesh axis runs over, the one named last changes fastest.
Arguments:
- dosage: bfloat16 [131072, 1024], P('samp', 'snp'), may hold values from -6 to 6
- pair_row: int32 [64, 4, 4096], P('samp'), may hold values from 0 to 2047
- pair_col: int32 [64, 4, 4096], P('samp'), may hold values from 0 to 2047
- pair_count: int32 [64, 4], P('samp'), may hold values from 512 to 4096, as said below
Outputs:
- sparse_grm: float32 [64, 4, 4096], P('samp', None, 'snp')
Inputs may be any that keep to these rules, and one draw needn't show every extreme that they name: pair_count[b, s] is the number of leading live slots of block b at distance s; the largest, 4096, occurs in every draw.
All inputs are finite; a program needn't handle non-finite values.
Results may differ from a plain program's by a relative error of at most 0.0003.
Values may be sent and summed in bfloat16 or wider, within the bound.
A program may use at most 128 MiB of HBM per device.

v0:
```python
import jax
import jax.numpy as jnp
from jax import lax
from jax.sharding import PartitionSpec as P

SNPS = 1024
STOPS = 4


def from_behind(block, axis, distance):
    devices = range(lax.axis_size(axis))
    route = [((i - distance) % len(devices), i) for i in devices]
    return lax.ppermute(block, axis, route)


def row_terms(own_block, peer_block, pair_rows, pair_cols):
    width = own_block.shape[0]
    tile = lax.dot_general(
        own_block, peer_block, (((1,), (1,)), ((), ())), preferred_element_type=jnp.float32
    )
    flat_index = pair_rows * width + pair_cols
    return jnp.take(tile.reshape(-1), flat_index, axis=0)


def shards(dosage, pair_row, pair_col, pair_count):
    row_lists = pair_row[0]
    col_lists = pair_col[0]
    live_count = pair_count[0]
    slots = row_lists.shape[1]
    live_mask = jnp.arange(slots, dtype=jnp.int32)[None, :] < live_count[:, None]
    peer_block = dosage
    term_list = []
    for stop_index in range(STOPS):
        if stop_index > 0:
            peer_block = from_behind(peer_block, "samp", 1)
        partial_sums = row_terms(dosage, peer_block, row_lists[stop_index], col_lists[stop_index])
        stop_term = jnp.where(live_mask[stop_index], partial_sums, jnp.zeros_like(partial_sums))
        term_list.append(lax.psum_scatter(stop_term, "snp", scatter_dimension=0, tiled=True))
    shares = jnp.stack(term_list)
    return (shares / SNPS)[None]


def solution(mesh):
    in_specs = (P("samp", "snp"), P("samp", None, None), P("samp", None, None), P("samp", None))
    out_specs = P("samp", None, "snp")
    return jax.shard_map(shards, mesh=mesh, in_specs=in_specs, out_specs=out_specs, check_vma=False)
```

profile of v0, /device:TPU:0, one launch (start us, length us, event | category | flops | bytes accessed | tf_op | source)
XLA Modules:
  0.0 353.7 jit_solution(1290254335093690786)
XLA Ops:
  6.5 1.2 slice_add_fusion.3
  7.8 31.1 %collective-permute-done = bf16[2048,512]{1,0:T(8,128)(2,1)S(1)} collective-permute-done((bf16[2048,512]{1,0:T(8,128)(2,1)}, bf16[2048,512]{1,0:T(8,128)(2,1)S(1)}, u32[]{:S(2)}, u32[]{:S(2)}) %collective-permute-start) | collective-permute-done | bytes 2097184 | tf_op jit(solution)/shard_map/ppermute | solution.py:13
  38.9 7.8 %convolution_bitcast_fusion.3 = f32[256,16,8,128]{3,2,1,0:T(8,128)S(1)} fusion(bf16[2048,512]{1,0:T(8,128)(2,1)} %param.6), kind=kOutput, calls=%fused_computation.7 | convolution fusion | flops 4294967296 | bytes 18874368 | tf_op jit(solution)/shard_map/dot_general | solution.py:18
  46.8 23.4 %collective-permute-done.1 = bf16[2048,512]{1,0:T(8,128)(2,1)} collective-permute-done((bf16[2048,512]{1,0:T(8,128)(2,1)S(1)}, bf16[2048,512]{1,0:T(8,128)(2,1)}, u32[]{:S(2)}, u32[]{:S(2)}) %collective-permute-start.1) | collective-permute-done | bytes 2097184 | tf_op jit(solution)/shard_map/ppermute | solution.py:13
  70.3 7.5 %copy.5 = f32[256,16,8,128]{3,1,2,0:T(8,128)} copy(f32[256,16,8,128]{3,2,1,0:T(8,128)S(1)} %convolution_bitcast_fusion.3) | data formatting | bytes 33554432
  77.8 48.5 %gather_fusion = f32[4096]{0:T(1024)S(1)} fusion(f32[4194304]{0:T(1024)} %bitcast.30, s32[4096]{0:T(1024)S(1)} %fusion), kind=kCustom, calls=%fused_computation.clone | custom fusion | bytes 49152 | tf_op jit(solution)/shard_map/jit(_take)/gather | solution.py:22
  126.4 6.4 %convolution_bitcast_fusion.2 = f32[256,16,8,128]{3,2,1,0:T(8,128)S(1)} fusion(bf16[2048,512]{1,0:T(8,128)(2,1)S(1)} %copy-done.1, bf16[2048,512]{1,0:T(8,128)(2,1)} %copy-done.2), kind=kOutput, calls=%fused_computation.6 | convolution fusion | flops 4294967296 | bytes 20971520 | tf_op jit(solution)/shard_map/dot_general | solution.py:18
  132.8 7.5 %copy.6 = f32[256,16,8,128]{3,1,2,0:T(8,128)} copy(f32[256,16,8,128]{3,2,1,0:T(8,128)S(1)} %convolution_bitcast_fusion.2) | data formatting | bytes 33554432
  140.3 48.4 %gather_fusion.1 = f32[4096]{0:T(1024)S(1)} fusion(f32[4194304]{0:T(1024)} %bitcast.31, s32[4096]{0:T(1024)S(1)} %fusion.1), kind=kCustom, calls=%fused_computation.1.clone | custom fusion | bytes 49152 | tf_op jit(solution)/shard_map/jit(_take)/gather | solution.py:22
  188.7 0.6 select_select_fusion.2
  189.3 6.4 %convolution_bitcast_fusion.1 = f32[256,16,8,128]{3,2,1,0:T(8,128)S(1)} fusion(bf16[2048,512]{1,0:T(8,128)(2,1)S(1)} %copy-done.1, bf16[2048,512]{1,0:T(8,128)(2,1)} %collective-permute-done.1), kind=kOutput, calls=%fused_computation.5 | convolution fusion | flops 4294967296 | bytes 20971520 | tf_op jit(solution)/shard_map/dot_general | solution.py:18
  195.7 7.7 %copy.7 = f32[256,16,8,128]{3,1,2,0:T(8,128)} copy(f32[256,16,8,128]{3,2,1,0:T(8,128)S(1)} %convolution_bitcast_fusion.1) | data formatting | bytes 33554432
  203.4 48.4 %gather_fusion.2 = f32[4096]{0:T(1024)S(1)} fusion(f32[4194304]{0:T(1024)} %bitcast.32, s32[4096]{0:T(1024)S(1)} %fusion.2), kind=kCustom, calls=%fused_computation.2.clone | custom fusion | bytes 49152 | tf_op jit(solution)/shard_map/jit(_take)/gather | solution.py:22
  251.9 6.4 %convolution_bitcast_fusion = f32[256,16,8,128]{3,2,1,0:T(8,128)S(1)} fusion(bf16[2048,512]{1,0:T(8,128)(2,1)S(1)} %copy-done.1, bf16[2048,512]{1,0:T(8,128)(2,1)} %collective-permute-done.2), kind=kOutput, calls=%fused_computation.4 | convolution fusion | flops 4294967296 | bytes 20971520 | tf_op jit(solution)/shard_map/dot_general | solution.py:18
  258.3 7.5 %copy.8 = f32[256,16,8,128]{3,1,2,0:T(8,128)} copy(f32[256,16,8,128]{3,2,1,0:T(8,128)S(1)} %convolution_bitcast_fusion) | data formatting | bytes 33554432
  265.8 48.4 %gather_fusion.3 = f32[4096]{0:T(1024)S(1)} fusion(f32[4194304]{0:T(1024)} %bitcast.33, s32[4096]{0:T(1024)S(1)} %fusion.3), kind=kCustom, calls=%fused_computation.3.clone | custom fusion | bytes 49152 | tf_op jit(solution)/shard_map/jit(_take)/gather | solution.py:22
  314.2 0.6 select_select_fusion
  314.9 0.7 dynamic-slice
  316.2 27.2 %all-reduce.7.cloned.1.call-done = (f32[4096]{0:T(1024)}, f32[4096]{0:T(1024)}, f32[4096]{0:T(1024)}, f32[4096]{0:T(1024)}) async-done(((f32[4096]{0:T(1024)}, f32[4096]{0:T(1024)}, f32[4096]{0:T(1024)}, f32[4096]{0:T(1024)}), (f32[4096]{0:T(1024)}, f32[4096]{0:T(1024)}, f32[4096]{0:T(1024)}, f32[4096]{0:T(1024)})) %all-reduce.7.cloned.1.call-update) | async-done | bytes 65552
  343.4 0.7 dynamic-slice.7
  344.1 0.7 dynamic-slice.5
  344.8 0.7 dynamic-slice.3
  345.5 0.7 dynamic-slice.1
  346.2 0.7 maximum_multiply_fusion
  (20 shorter events, 0.4 us)
Async XLA Ops:
  6.5 336.8 %all-reduce.7.cloned.1.call-start = ((), (), s32[]{:S(2)}) async-start(), calls=%async_computation | async-start | bytes 131072
  6.5 32.3 %collective-permute-start = (bf16[2048,512]{1,0:T(8,128)(2,1)}, bf16[2048,512]{1,0:T(8,128)(2,1)S(1)}, u32[]{:S(2)}, u32[]{:S(2)}) collective-permute-start(bf16[2048,512]{1,0:T(8,128)(2,1)} %param.6), channel_id=1, source_target_pairs={{126,0},{0,2},{2,4},{4,6},{6,8},{8,10},{10,12},{12,14},{14,16},{16... | collective-permute-start | bytes 6291464 | tf_op jit(solution)/shard_map/ppermute | solution.py:13
  38.9 7.8 %copy-start.2 = (bf16[2048,512]{1,0:T(8,128)(2,1)}, bf16[2048,512]{1,0:T(8,128)(2,1)S(1)}, u32[]{:S(2)}) copy-start(bf16[2048,512]{1,0:T(8,128)(2,1)S(1)} %collective-permute-done) | copy-start | bytes 6291460
  38.9 31.3 %collective-permute-start.1 = (bf16[2048,512]{1,0:T(8,128)(2,1)S(1)}, bf16[2048,512]{1,0:T(8,128)(2,1)}, u32[]{:S(2)}, u32[]{:S(2)}) collective-permute-start(bf16[2048,512]{1,0:T(8,128)(2,1)S(1)} %collective-permute-done), channel_id=1, source_target_pairs={{126,0},{0,2},{2,4},{4,6},{6,8},{8,10},{10,12},{12,14},{14,16},{16... | collective-permute-start | bytes 6291464 | tf_op jit(solution)/shard_map/ppermute | solution.py:13
  38.9 7.8 %copy-start = (s32[1,4]{1,0:T(1,128)S(1)}, s32[1,4]{1,0:T(1,128)}, u32[]{:S(2)}) copy-start(s32[1,4]{1,0:T(1,128)} %param.9) | copy-start | bytes 52
  70.1 181.7 %collective-permute-start.2 = (bf16[2048,512]{1,0:T(8,128)(2,1)}, bf16[2048,512]{1,0:T(8,128)(2,1)}, u32[]{:S(2)}, u32[]{:S(2)}) collective-permute-start(bf16[2048,512]{1,0:T(8,128)(2,1)} %collective-permute-done.1), channel_id=1, source_target_pairs={{126,0},{0,2},{2,4},{4,6},{6,8},{8,10},{10,12},{12,14},{14,16},{16... | collective-permute-start | bytes 6291464 | tf_op jit(solution)/shard_map/ppermute | solution.py:13
  77.8 48.6 %copy-start.1 = (bf16[2048,512]{1,0:T(8,128)(2,1)S(1)}, bf16[2048,512]{1,0:T(8,128)(2,1)}, u32[]{:S(2)}) copy-start(bf16[2048,512]{1,0:T(8,128)(2,1)} %param.6) | copy-start | bytes 6291460
  265.8 49.1 %copy-start.3 = (u32[128]{0:T(128)S(1)}, u32[128]{0:T(128)}, u32[]{:S(2)}) copy-start(u32[128]{0:T(128)} %constant.22) | copy-start | bytes 1540
Sparse Core Ops, SparseCore 0:
  315.0 28.3 all-reduce.6
where the time goes:
time: 361 us; the launch traced here: 354 us
  local copies, waits for them, and re-layouts  228 us (63%)
  waiting for transfers between devices  81.6 us (23%)
  matrix products  26.9 us (7%)
  between operations  14.2 us (4%)
    gather x4, local copies, waits for them, and re-layouts, row_terms(): return jnp.take(tile.reshape(-1), flat_index, axis=0)  194 us
    ppermute x3, waiting for transfers between devices, from_behind(): return lax.ppermute(block, axis, route)  54.5 us
    unnamed x17, local copies, waits for them, and re-layouts  33.7 us
    unnamed x2, waiting for transfers between devices  27.2 us
    dot_general x4, matrix products, row_terms(): lax.dot_general(own_block, peer_block, (((1,), (1,)), ((), ())), preferre...  26.9 us
  transfers between devices with their start and end apart: 4, of which 3 were waited for; matrix products, arithmetic and copies ran while one was open for 54% of the time, Pallas kernels for 0%

commit v1 on v0

v1 whole, which is shorter than its diff:
```python
import jax
import jax.numpy as jnp
from jax import lax
from jax.experimental import pallas as pl
from jax.experimental.pallas import tpu as pltpu
from jax.sharding import PartitionSpec as P

MESH = pl.DeviceIdType.MESH

BLK = 2048
HALF = 512
SNPS = 1024
STOPS = 4
PAIRS = 4096
NBLK = 64
CHUNKS = 8
CHUNK = BLK // CHUNKS
LIST = PAIRS // 128
SHARE = LIST // 2

OWN, ODD, EVEN, THIRD = 0, 1, 2, 3


def kernel(x, row_hbm, col_hbm, out, buf, tile0, tile1, row_v, col_v, addr_v, lane_v, addr_s, sums, land,
           own_sem, list_sem, addr_sem,
           odd_send, odd_recv, even_send, even_recv, third_send, third_recv, pass_send,
           ask_send, ask_recv, part_send, part_recv):
    samp = lax.axis_index("samp")
    snp = lax.axis_index("snp")
    core = lax.rem(samp, 2)
    chip = samp // 2
    even_core = core == 0
    odd_core = core == 1

    def device(chip_step, to_core, to_snp):
        to_chip = lax.rem(chip + (chip_step + NBLK // 2), NBLK // 2)
        return {"samp": to_chip * 2 + to_core, "snp": to_snp}

    sibling = device(0, 1 - core, snp)
    partner = device(0, core, 1 - snp)

    barrier = pltpu.get_barrier_semaphore()
    greeted = [sibling, partner]
    for chip_step in (-1, 1):
        for to_core in (0, 1):
            for to_snp in (snp, 1 - snp):
                greeted.append(device(chip_step, to_core, to_snp))
    for other in greeted:
        pl.semaphore_signal(barrier, inc=1, device_id=other, device_id_type=MESH)
    pl.semaphore_wait(barrier, len(greeted))

    def rows_of(n):
        return pl.ds(pl.multiple_of(n * CHUNK, CHUNK), CHUNK)

    def send_odd(n):
        return pltpu.make_async_remote_copy(
            x.at[rows_of(n)], buf.at[ODD, rows_of(n)], odd_send.at[n], odd_recv.at[n],
            device_id=device(1, 0, snp), device_id_type=MESH)

    def send_even(n):
        return pltpu.make_async_remote_copy(
            x.at[rows_of(n)], buf.at[EVEN, rows_of(n)], even_send.at[n], even_recv.at[n],
            device_id=device(1, 1, snp), device_id_type=MESH)

    def pass_odd(n):
        return pltpu.make_async_remote_copy(
            buf.at[ODD, rows_of(n)], buf.at[ODD, rows_of(n)], pass_send.at[n], odd_recv.at[n],
            device_id=sibling, device_id_type=MESH)

    def pass_even(n):
        return pltpu.make_async_remote_copy(
            buf.at[EVEN, rows_of(n)], buf.at[EVEN, rows_of(n)], pass_send.at[n], even_recv.at[n],
            device_id=sibling, device_id_type=MESH)

    def send_third(k):
        return pltpu.make_async_remote_copy(
            x, buf.at[THIRD], third_send.at[k], third_recv,
            device_id=device(-1, 0, snp) if k == 0 else sibling, device_id_type=MESH)

    @pl.when(odd_core)
    def _():
        for n in range(CHUNKS):
            send_odd(n).start()

    @pl.when(even_core)
    def _():
        send_third(0).start()
        send_third(1).start()

    load_own = pltpu.make_async_copy(x, buf.at[OWN], own_sem)
    load_own.start()
    load_row = pltpu.make_async_copy(row_hbm.at[0], row_v, list_sem.at[0])
    load_col = pltpu.make_async_copy(col_hbm.at[0], col_v, list_sem.at[1])
    load_row.start()
    load_col.start()
    load_row.wait()
    load_col.wait()

    distance = lax.broadcasted_iota(jnp.int32, (STOPS, 128), 0)
    swap = (distance == 3) & jnp.broadcast_to(even_core, (STOPS, 128))
    for k in range(LIST):
        rows = row_v[:, k * 128:(k + 1) * 128]
        cols = col_v[:, k * 128:(k + 1) * 128]
        down = jnp.where(swap, cols, rows)
        across = jnp.where(swap, rows, cols)
        address = (across >> 7) * BLK + down
        lanes = across & 127
        for s in range(STOPS):
            addr_v[s * LIST + k:s * LIST + k + 1, :] = address[s:s + 1, :]
            lane_v[s * LIST + k:s * LIST + k + 1, :] = lanes[s:s + 1, :]

    own_addr = pltpu.make_async_copy(addr_v.at[pl.ds(0, 4 * LIST)], addr_s.at[pl.ds(0, 4 * LIST)], addr_sem.at[0])
    own_addr.start()
    third_list = pl.ds(3 * LIST, LIST)
    asked_list = pl.ds(4 * LIST, LIST)
    ask = [
        pltpu.make_async_remote_copy(v.at[third_list], v.at[asked_list], ask_send.at[i], ask_recv.at[i],
                                     device_id=device(-1, 0, snp), device_id_type=MESH)
        for i, v in enumerate((addr_v, lane_v))
    ]

    @pl.when(even_core)
    def _():
        for copy in ask:
            copy.start()

    load_own.wait()
    own_addr.wait()

    lane_iota = lax.broadcasted_iota(jnp.int32, (8, 128), 1)
    sub_iota = lax.broadcasted_iota(jnp.int32, (8, 128), 0)
    tiles = (tile0, tile1)

    def multiply(lhs, rhs, tile, n):
        product = lax.dot_general(
            buf[lhs], buf[rhs, rows_of(n)], (((1,), (1,)), ((), ())), preferred_element_type=jnp.float32)
        tile[pl.ds(pl.multiple_of(n * 2 * BLK, BLK), BLK), :] = product[:, :128]
        tile[pl.ds(pl.multiple_of(n * 2 * BLK + BLK, BLK), BLK), :] = product[:, 128:]

    def read_out(tile, listed, into, n):
        group, first = n // 2, lax.rem(n, 2) * 64
        at = listed * LIST + group * 8
        lanes = lane_v[pl.ds(pl.multiple_of(at, 8), 8), :]
        slots = addr_s.at[pl.ds(at, 8)]
        found = jnp.zeros((8, 128), jnp.float32)
        for k in range(64):
            rows = None
            for s in range(8):
                one = jnp.broadcast_to(tile[pl.ds(slots[s, first + k], 1), :], (8, 128))
                rows = one if rows is None else jnp.where(sub_iota == s, one, rows)
            picked = jnp.take_along_axis(rows, lanes, axis=1)
            found = jnp.where(lane_iota == first + k, picked, found)
        here = pl.ds(pl.multiple_of(group * 8, 8), 8)
        mine = (lane_iota >= first) & (lane_iota < first + 64)
        sums[into, here, :] = jnp.where(mine, found, sums[into, here, :])

    def send_part(step, s, to, half, place):
        return pltpu.make_async_remote_copy(
            sums.at[step, pl.ds(pl.multiple_of(half * SHARE, SHARE), SHARE)], land.at[place, s],
            part_send.at[step, place], part_recv.at[place, s], device_id=to, device_id_type=MESH)

    def even_s(step):
        return (0, 1, 3, 2)[step]

    def send_sums(step):
        @pl.when(odd_core)
        def _():
            land[0, step] = sums[step, pl.ds(pl.multiple_of(snp * SHARE, SHARE), SHARE), :]
            send_part(step, step, partner, 1 - snp, 1).start()

        @pl.when(even_core)
        def _():
            s = even_s(step)
            if s == 3:
                send_part(step, 3, device(1, 0, snp), snp, 0).start()
                send_part(step, 3, device(1, 0, 1 - snp), 1 - snp, 1).start()
            else:
                land[0, s] = sums[step, pl.ds(pl.multiple_of(snp * SHARE, SHARE), SHARE), :]
                send_part(step, s, partner, 1 - snp, 1).start()

    for step in range(STOPS + 1):
        lhs = rhs = 0
        if step == 1:
            rhs = jnp.where(even_core, ODD, THIRD)
        elif step == 2:
            lhs = jnp.where(even_core, ODD, OWN)
            rhs = jnp.where(even_core, THIRD, ODD)
        elif step == 3:
            rhs = EVEN
        listed = step - 1
        if step == 3:
            listed = jnp.where(even_core, 4, 2)
        elif step == 4:
            listed = jnp.where(even_core, 2, 3)

        if step == 1:
            @pl.when(odd_core)
            def _():
                send_third(1).wait_recv()
        if step == 2:
            @pl.when(even_core)
            def _():
                send_third(0).wait_recv()
                for copy in ask:
                    copy.wait_recv()
                asked = pltpu.make_async_copy(addr_v.at[asked_list], addr_s.at[asked_list], addr_sem.at[1])
                asked.start()
                asked.wait()

        @pl.loop(0, CHUNKS)
        def _(n):
            if step == 1:
                @pl.when(even_core)
                def _():
                    send_odd(n).wait_recv()
                    pass_odd(n).start()

                @pl.when(even_core & (n == CHUNKS - 2))
                def _():
                    for m in range(CHUNKS):
                        send_even(m).start()
            if step == 2:
                @pl.when(odd_core)
                def _():
                    pass_odd(n).wait_recv()
            if step == 3:
                send_even(n).wait_recv()

                @pl.when(odd_core)
                def _():
                    pass_even(n).start()
            if step < STOPS:
                multiply(lhs, rhs, tiles[step % 2], n)
            if step > 0:
                read_out(tiles[(step - 1) % 2], listed, step - 1, n)
        if step > 0:
            send_sums(step - 1)

    @pl.when(odd_core)
    def _():
        for n in range(CHUNKS):
            send_odd(n).wait_send()
            pass_even(n).wait_send()
        for step in range(STOPS):
            send_part(step, step, partner, 1 - snp, 1).wait()

    @pl.when(even_core)
    def _():
        for n in range(CHUNKS):
            send_even(n).wait_send()
            pass_odd(n).wait_send()
        send_third(0).wait_send()
        send_third(1).wait_send()
        for copy in ask:
            copy.wait_send()
        for step in range(STOPS):
            s = even_s(step)
            if s == 3:
                send_part(step, 3, device(1, 0, snp), snp, 0).wait()
                send_part(step, 3, device(1, 0, 1 - snp), 1 - snp, 1).wait()
            else:
                send_part(step, s, partner, 1 - snp, 1).wait()

    for s in range(STOPS):
        both = land[0, s] + land[1, s]
        for k in range(SHARE):
            out[0, s:s + 1, k * 128:(k + 1) * 128] = both[k:k + 1, :]


def shards(dosage, pair_row, pair_col, pair_count):
    dma = pltpu.SemaphoreType.DMA
    sums = pl.pallas_call(
        kernel,
        out_shape=jax.ShapeDtypeStruct((1, STOPS, PAIRS // 2), jnp.float32),
        in_specs=[pl.BlockSpec(memory_space=pl.ANY)] * 3,
        out_specs=pl.BlockSpec(memory_space=pltpu.VMEM),
        scratch_shapes=[
            pltpu.VMEM((4, BLK, HALF), jnp.bfloat16),
            pltpu.VMEM((BLK * 16, 128), jnp.float32),
            pltpu.VMEM((BLK * 16, 128), jnp.float32),
            pltpu.VMEM((STOPS, PAIRS), jnp.int32),
            pltpu.VMEM((STOPS, PAIRS), jnp.int32),
            pltpu.VMEM((5 * LIST, 128), jnp.int32),
            pltpu.VMEM((5 * LIST, 128), jnp.int32),
            pltpu.SMEM((5 * LIST, 128), jnp.int32),
            pltpu.VMEM((STOPS, LIST, 128), jnp.float32),
            pltpu.VMEM((2, STOPS, SHARE, 128), jnp.float32),
            dma, dma((2,)), dma((2,)),
            dma((CHUNKS,)), dma((CHUNKS,)), dma((CHUNKS,)), dma((CHUNKS,)), dma((2,)), dma, dma((CHUNKS,)),
            dma((2,)), dma((2,)), dma((STOPS, 2)), dma((2, STOPS)),
        ],
        compiler_params=pltpu.CompilerParams(
            collective_id=0, has_side_effects=True, vmem_limit_bytes=56 << 20),
        cost_estimate=pl.CostEstimate(
            flops=2 * STOPS * BLK * BLK * HALF, bytes_accessed=2 * BLK * HALF * 2, transcendentals=0),
    )(dosage, pair_row, pair_col)
    slot = lax.axis_index("snp") * (PAIRS // 2) + jnp.arange(PAIRS // 2, dtype=jnp.int32)
    live = slot[None, None, :] < pair_count[:, :, None]
    return jnp.where(live, sums / SNPS, jnp.zeros_like(sums))


def solution(mesh):
    in_specs = (P("samp", "snp"), P("samp", None, None), P("samp", None, None), P("samp", None))
    out_specs = P("samp", None, "snp")
    return jax.shard_map(shards, mesh=mesh, in_specs=in_specs, out_specs=out_specs, check_vma=False)
```

time: 361 us -> 69.2 us (0.19); the launches traced: 354 us -> 68.7 us
  local copies, waits for them, and re-layouts: 228 us -> 0.01 us
  waiting for transfers between devices: 81.6 us -> 0 us
  Pallas kernels: 0 us -> 67.3 us
  matrix products: 26.9 us -> 0 us
  between operations: 14.2 us -> 0.02 us
    gather x4 -> x0, local copies, waits for them, and re-layouts: 194 us -> none  [row_terms(): return jnp.take(tile.reshape(-1), flat_index, axis=0)]
    pallas_call x0 -> x1, Pallas kernels: none -> 67.3 us  [shards(): pl.pallas_call(kernel, out_shape=jax.ShapeDtypeStruct((1, STOPS, PAIRS //...]
    ppermute x3 -> x0, waiting for transfers between devices: 54.5 us -> none  [from_behind(): return lax.ppermute(block, axis, route)]
    unnamed x17 -> x2, local copies, waits for them, and re-layouts: 33.7 us -> 0.01 us
    unnamed x2 -> x0, waiting for transfers between devices: 27.2 us -> none
    dot_general x4 -> x0, matrix products: 26.9 us -> none  [row_terms(): lax.dot_general(own_block, peer_block, (((1,), (1,)), ((), ())), preferre...]
  transfers between devices with their start and end apart: 4 -> 0, of which waited for: 3 -> 0; matrix products, arithmetic and copies ran while one was open for 54% -> 0% of each run, Pallas kernels for 0% -> 0%
where the time goes in v1:
time: 69.2 us; the launch traced here: 68.7 us
  Pallas kernels  67.3 us (97%)
  other arithmetic  1.45 us (2%)
    pallas_call x1, Pallas kernels, shards(): pl.pallas_call(kernel, out_shape=jax.ShapeDtypeStruct((1, STOPS, PAIRS //...  67.3 us
    select_n x1, other arithmetic, shards(): return jnp.where(live, sums / SNPS, jnp.zeros_like(sums))  1.45 us

profile of v1, /device:TPU:0, one launch (start us, length us, event | category | flops | bytes accessed | tf_op | source)
XLA Modules:
  0.0 68.7 jit_solution(3077911296095954652)
XLA Ops:
  0.0 0.0 copy-start
  0.0 67.3 %shard_map.49 = f32[1,4,2048]{2,1,0:T(4,128)} custom-call(bf16[2048,512]{1,0:T(8,128)(2,1)} %x.1, s32[1,4,4096]{2,1,0:T(4,128)} %row_hbm.1, s32[1,4,4096]{2,1,0:T(4,128)} %col_hbm.1), custom_call_target="tpu_custom_call" | custom-call | flops 17179869184 | bytes 4194304 | tf_op jit(solution)/shard_map/pallas_call | solution.py:272
  67.3 0.0 copy-done
  67.3 1.4 %multiply_select_fusion = f32[1,4,2048]{2,1,0:T(4,128)} fusion(f32[1,4,2048]{2,1,0:T(4,128)} %shard_map.49, s32[2048]{0:T(1024)S(1)} %iota_add_fusion, s32[4]{0:T(128)S(1)} %bitcast.1), kind=kLoop, calls=%fused_computation | loop fusion | flops 24576 | bytes 73744 | tf_op jit(solution)/shard_map/jit(_where)/select_n | solution.py:299
  (1 shorter events, 0.0 us)
Async XLA Ops:
  0.0 67.3 %copy-start = (s32[1,4]{1,0:T(1,128)S(1)}, s32[1,4]{1,0:T(1,128)}, u32[]{:S(2)}) copy-start(s32[1,4]{1,0:T(1,128)} %param.7) | copy-start | bytes 52

commit v2 on v0

v2 whole, which is shorter than its diff:
```python
import jax
import jax.numpy as jnp
from jax import lax
from jax.experimental import pallas as pl
from jax.experimental.pallas import tpu as pltpu
from jax.sharding import PartitionSpec as P

MESH = pl.DeviceIdType.MESH

BLK = 2048
HALF = 512
QUARTER = 256
SNPS = 1024
STOPS = 4
PAIRS = 4096
CHIPS = 32
CHUNKS = 8
CHUNK = BLK // CHUNKS
LIST = PAIRS // 128
SHARE = LIST // 2
ROWS = LIST // CHUNKS
STEPS = 5
UNROLL = 2

OWN, LEFT, RIGHT, OTHER = 0, 1, 2, 3
LISTS = STOPS + 2


def kernel(x, row_hbm, col_hbm, out, buf, quart, own_quart, tile0, tile1, row_v, col_v, pair_v, addr_v, lane_v, slots0, slots1, sums, land,
           own_sem, list_sem, addr_sem, main_send, main_recv, pass_send, pass_recv, quart_send, quart_recv,
           sib_send, sib_recv, ask_send, ask_recv, part_send, part_recv):
    samp = lax.axis_index("samp")
    snp = lax.axis_index("snp")
    core = lax.rem(samp, 2)
    chip = samp // 2
    even_core = core == 0
    odd_core = core == 1

    def device(chip_step, to_core, to_snp):
        to_chip = lax.rem(chip + (chip_step + CHIPS), CHIPS)
        return {"samp": to_chip * 2 + to_core, "snp": to_snp}

    sibling = device(0, 1 - core, snp)
    ahead = 2 * core - 1
    main_to = device(ahead, 1 - core, snp)
    quart_to = device(-ahead, 1 - core, snp)

    barrier = pltpu.get_barrier_semaphore()
    greeted = [sibling, device(0, core, 1 - snp), device(0, 1 - core, 1 - snp)]
    for chip_step in (-1, 1):
        for to_core in (0, 1):
            for to_snp in (snp, 1 - snp):
                greeted.append(device(chip_step, to_core, to_snp))
    for other in greeted:
        pl.semaphore_signal(barrier, inc=1, device_id=other, device_id_type=MESH)
    pl.semaphore_wait(barrier, len(greeted))

    def rows_of(n):
        return pl.ds(pl.multiple_of(n * CHUNK, CHUNK), CHUNK)

    def send_main(n):
        return pltpu.make_async_remote_copy(
            x.at[rows_of(n)], buf.at[jnp.where(even_core, LEFT, RIGHT), rows_of(n)], main_send.at[n], main_recv.at[n],
            device_id=main_to, device_id_type=MESH)

    def pass_on(n):
        return pltpu.make_async_remote_copy(
            buf.at[RIGHT, rows_of(n)], buf.at[RIGHT, rows_of(n)], pass_send.at[n], pass_recv.at[n],
            device_id=sibling, device_id_type=MESH)

    def send_quarter(n):
        columns = pl.ds(pl.multiple_of(core * QUARTER, QUARTER), QUARTER)
        return pltpu.make_async_remote_copy(
            x.at[rows_of(n), columns], quart.at[rows_of(n)], quart_send.at[n], quart_recv.at[n],
            device_id=quart_to, device_id_type=MESH)

    send_sib = pltpu.make_async_remote_copy(
        x, buf.at[jnp.where(even_core, OTHER, LEFT)], sib_send, sib_recv, device_id=sibling, device_id_type=MESH)

    load_own = pltpu.make_async_copy(x, buf.at[OWN], own_sem)
    load_row = pltpu.make_async_copy(row_hbm.at[0], row_v, list_sem.at[0])
    load_col = pltpu.make_async_copy(col_hbm.at[0], col_v, list_sem.at[1])
    load_part = pltpu.make_async_copy(
        x.at[:, pl.ds(pl.multiple_of((1 - core) * QUARTER, QUARTER), QUARTER)], own_quart, list_sem.at[2])
    load_own.start()
    send_sib.start()
    for n in range(CHUNKS):
        send_main(n).start()
    load_row.start()
    load_col.start()
    load_part.start()
    def ask(i):
        to = device(-1, 1 - core, snp) if i == 1 else device(core - 1, 1 - core, snp)
        return pltpu.make_async_remote_copy(
            pair_v.at[pl.ds((2 + i) * LIST, LIST)], pair_v.at[pl.ds((4 + i) * LIST, LIST)], ask_send.at[i], ask_recv.at[i],
            device_id=to, device_id_type=MESH)

    slots = (slots0, slots1)

    def load_slots(step):
        return pltpu.make_async_copy(
            addr_v.at[pl.ds(step * LIST, UNROLL * ROWS)], slots[step % 2], addr_sem.at[step % 2, 0])

    def reload_slots(step, m, n):
        return pltpu.make_async_copy(
            addr_v.at[pl.ds(step * LIST + ((m + 1) * UNROLL + n) * ROWS, ROWS)], slots[step % 2].at[pl.ds(n * ROWS, ROWS)],
            addr_sem.at[step % 2, 1 + n])

    def prepare(step):
        listed = (0, 0, jnp.where(even_core, 1, 4), jnp.where(even_core, 4, 5), jnp.where(even_core, 5, 3))[step]
        if step == 1:
            listed = jnp.where(even_core, 0, 1)
        swapped = {2: odd_core, 4: even_core}.get(step)
        for group in range(LIST // 8):
            pairs = pair_v[pl.ds(pl.multiple_of(listed * LIST + group * 8, 8), 8), :]
            down, across = pairs >> 11, pairs & (BLK - 1)
            if swapped is not None:
                swap = jnp.broadcast_to(swapped, (8, 128))
                down, across = jnp.where(swap, across, down), jnp.where(swap, down, across)
            here = slice(step * LIST + group * 8, step * LIST + group * 8 + 8)
            addr_v[here, :] = (across >> 7) * BLK + down
            lanes = across & 127
            turned = pltpu.roll(lanes, 64, 1)
            at = (step * LIST + group * 8) * 2
            for i in range(2):
                lane_v[at + 8 * i:at + 8 * i + 4, :] = lanes[4 * i:4 * i + 4, :]
                lane_v[at + 8 * i + 4:at + 8 * i + 8, :] = turned[4 * i:4 * i + 4, :]


    def read_lists():
        load_row.wait()
        load_col.wait()

        for k in range(LIST):
            pairs = row_v[:, k * 128:(k + 1) * 128] * BLK + col_v[:, k * 128:(k + 1) * 128]
            for s in range(STOPS):
                pair_v[s * LIST + k:s * LIST + k + 1, :] = pairs[s:s + 1, :]
        ask(0).start()
        ask(1).start()
        prepare(0)
        load_slots(0).start()
        prepare(1)

    load_own.wait()

    lane_iota = lax.broadcasted_iota(jnp.int32, (8, 128), 1)
    sub_iota = lax.broadcasted_iota(jnp.int32, (8, 128), 0)
    tiles = (tile0, tile1)

    def multiply(step, n, on_core=None):
        tile = tiles[step % 2]
        if step == 0:
            lhs, rhs = buf[OWN], buf[OWN, rows_of(n)]
        elif step == 1:
            lhs, rhs = buf[OWN], buf[OTHER, rows_of(n)]
        elif step == 2 and on_core == 0:
            lhs, rhs = buf[OWN], buf[RIGHT, rows_of(n)]
        elif step == 2:
            lhs, rhs = buf[OTHER], buf[LEFT, rows_of(n)]
        elif step == 3:
            lhs, rhs = buf[LEFT], buf[RIGHT, rows_of(n)]
        else:
            lhs, rhs = own_quart[...], quart[rows_of(n)]
        product = lax.dot_general(lhs, rhs, (((1,), (1,)), ((), ())), preferred_element_type=jnp.float32)
        tile[pl.ds(pl.multiple_of(n * 2 * BLK, BLK), BLK), :] = product[:, :128]
        tile[pl.ds(pl.multiple_of(n * 2 * BLK + BLK, BLK), BLK), :] = product[:, 128:]

    def read_out(step, n, q):
        tile, here = tiles[step % 2], slots[step % 2]
        lanes = lane_v[pl.ds(pl.multiple_of(step * LIST * 2 + n * 8, 8), 8), :]
        found = jnp.zeros((8, 128), jnp.float32)
        for k in range(64):
            rows = None
            for s in range(8):
                at = here[q * ROWS + s % ROWS, s // ROWS * 64 + k]
                one = jnp.broadcast_to(tile[pl.ds(at, 1), :], (8, 128))
                rows = one if rows is None else jnp.where(sub_iota == s, one, rows)
            picked = jnp.take_along_axis(rows, lanes, axis=1)
            found = jnp.where(lane_iota == k, picked, found)
        turned = pltpu.roll(found, 64, 1)
        sums[step, pl.ds(n * ROWS, ROWS), :] = jnp.where(lane_iota[:ROWS] < 64, found[:ROWS], turned[ROWS:])

    def share(step, half):
        return sums.at[step, pl.ds(pl.multiple_of(half * SHARE, SHARE), SHARE)]

    def send_part(step, half, to, place, s):
        return pltpu.make_async_remote_copy(
            share(step, half), land.at[place, s], part_send.at[step, place % 2], part_recv.at[place, s],
            device_id=to, device_id_type=MESH)

    even_parts = {0: (0, 0, None, 0), 2: (1, 0, None, 0), 3: (2, 0, 1, 0), 4: (3, 1, 1, 2)}
    odd_parts = {0: (0, 0, None, 0), 1: (1, 0, None, 0), 2: (2, 1, 0, 0), 3: (3, 1, 0, 0), 4: (3, 0, None, 0)}

    def part_copies(step, parts):
        s, chip_step, to_core, place = parts[step]
        if to_core is None:
            return [send_part(step, 1 - snp, device(0, core, 1 - snp), 1, s)]
        return [send_part(step, snp, device(chip_step, to_core, snp), place, s),
                send_part(step, 1 - snp, device(chip_step, to_core, 1 - snp), place + 1, s)]

    def hand_out(step):
        for own, parts in ((even_core, even_parts), (odd_core, odd_parts)):
            if step in parts:
                @pl.when(own)
                def _():
                    for copy in part_copies(step, parts):
                        copy.start()
                    if parts[step][2] is None:
                        land[0, parts[step][0]] = share(step, snp)[...]

    for step in range(STEPS + 1):
        if step == 1:
            read_lists()
            send_sib.wait_recv()
        if step == 2:
            ask(0).wait_recv()
            ask(1).wait_recv()
            for later in range(2, STEPS):
                prepare(later)
            for n in range(CHUNKS - 2):
                send_main(n).wait_send()
            for n in range(CHUNKS // 2):
                send_quarter(n).start()
        if step == 4:
            load_part.wait()
        if step > 0:
            load_slots(step - 1).wait()
        if 0 < step < STEPS:
            load_slots(step).start()

        @pl.loop(0, CHUNKS // UNROLL)
        def _(m):
            for q in range(UNROLL):
                n = m * UNROLL + q
                if step == 2:
                    send_main(n).wait_recv()

                    @pl.when(even_core)
                    def _():
                        pass_on(n).start()

                    if q == 0:
                        @pl.when(n == CHUNKS - UNROLL)
                        def _():
                            for i in range(CHUNKS // 2, CHUNKS):
                                send_quarter(i).start()
                if step == 3:
                    @pl.when(odd_core)
                    def _():
                        pass_on(n).wait_recv()
                if step == 4:
                    send_quarter(n).wait_recv()
                if step > 0:
                    @pl.when(m > 0)
                    def _():
                        reload_slots(step - 1, m - 1, q).wait()

                if step == 1:
                    @pl.when(odd_core)
                    def _():
                        multiply(step, n)
                        read_out(step - 1, n, q)

                    @pl.when(even_core)
                    def _():
                        read_out(step - 1, n, q)
                elif step == 2:
                    @pl.when(odd_core)
                    def _():
                        multiply(step, n)
                        read_out(step - 1, n, q)

                    @pl.when(even_core)
                    def _():
                        multiply(step, n, 0)
                elif 0 < step < STEPS:
                    @pl.when(core < 2)
                    def _():
                        multiply(step, n)
                        read_out(step - 1, n, q)
                elif step == 0:
                    multiply(step, n)
                else:
                    read_out(step - 1, n, q)

                if step > 0:
                    @pl.when(m < CHUNKS // UNROLL - 1)
                    def _():
                        reload_slots(step - 1, m, q).start()
        if step > 0:
            hand_out(step - 1)

    for n in range(CHUNKS):
        if n >= CHUNKS - 2:
            send_main(n).wait_send()
        send_quarter(n).wait_send()
    send_sib.wait_send()
    ask(0).wait_send()
    ask(1).wait_send()

    def landed(place, s):
        send_part(0, snp, sibling, place, s).wait_recv()

    for own, parts in ((even_core, even_parts), (odd_core, odd_parts)):
        @pl.when(own)
        def _():
            for step in parts:
                for copy in part_copies(step, parts):
                    copy.wait_send()
    for s in range(STOPS):
        landed(1, s)
    landed(0, 2)

    @pl.when(even_core)
    def _():
        for n in range(CHUNKS):
            pass_on(n).wait_send()
        landed(0, 3)

    @pl.when(odd_core)
    def _():
        landed(2, 3)
        landed(3, 3)
        land[0, 3] = land[0, 3] + (land[2, 3] + land[3, 3])

    for s in range(STOPS):
        both = land[0, s] + land[1, s]
        for k in range(SHARE):
            out[0, s:s + 1, k * 128:(k + 1) * 128] = both[k:k + 1, :]


def shards(dosage, pair_row, pair_col, pair_count):
    dma = pltpu.SemaphoreType.DMA
    sums = pl.pallas_call(
        kernel,
        out_shape=jax.ShapeDtypeStruct((1, STOPS, PAIRS // 2), jnp.float32),
        in_specs=[pl.BlockSpec(memory_space=pl.ANY)] * 3,
        out_specs=pl.BlockSpec(memory_space=pltpu.VMEM),
        scratch_shapes=[
            pltpu.VMEM((4, BLK, HALF), jnp.bfloat16),
            pltpu.VMEM((BLK, QUARTER), jnp.bfloat16),
            pltpu.VMEM((BLK, QUARTER), jnp.bfloat16),
            pltpu.VMEM((BLK * 16, 128), jnp.float32),
            pltpu.VMEM((BLK * 16, 128), jnp.float32),
            pltpu.VMEM((STOPS, PAIRS), jnp.int32),
            pltpu.VMEM((STOPS, PAIRS), jnp.int32),
            pltpu.VMEM((LISTS * LIST, 128), jnp.int32),
            pltpu.VMEM((STEPS * LIST, 128), jnp.int32),
            pltpu.VMEM((STEPS * LIST * 2, 128), jnp.int32),
            pltpu.SMEM((UNROLL * ROWS, 128), jnp.int32),
            pltpu.SMEM((UNROLL * ROWS, 128), jnp.int32),
            pltpu.VMEM((STEPS, LIST, 128), jnp.float32),
            pltpu.VMEM((4, STOPS, SHARE, 128), jnp.float32),
            dma, dma((3,)), dma((2, 1 + UNROLL)),
            dma((CHUNKS,)), dma((CHUNKS,)), dma((CHUNKS,)), dma((CHUNKS,)), dma((CHUNKS,)), dma((CHUNKS,)),
            dma, dma, dma((2,)), dma((2,)), dma((STEPS, 2)), dma((4, STOPS)),
        ],
        compiler_params=pltpu.CompilerParams(
            collective_id=0, has_side_effects=True, vmem_limit_bytes=56 << 20),
        cost_estimate=pl.CostEstimate(
            flops=2 * STOPS * BLK * BLK * HALF, bytes_accessed=2 * BLK * HALF * 2, transcendentals=0),
    )(dosage, pair_row, pair_col)
    slot = lax.axis_index("snp") * (PAIRS // 2) + jnp.arange(PAIRS // 2, dtype=jnp.int32)
    live = slot[None, None, :] < pair_count[:, :, None]
    return jnp.where(live, sums / SNPS, jnp.zeros_like(sums))


def solution(mesh):
    in_specs = (P("samp", "snp"), P("samp", None, None), P("samp", None, None), P("samp", None))
    out_specs = P("samp", None, "snp")
    return jax.shard_map(shards, mesh=mesh, in_specs=in_specs, out_specs=out_specs, check_vma=False)
```

time: 361 us -> 68.5 us (0.19); the launches traced: 354 us -> 68.3 us
  local copies, waits for them, and re-layouts: 228 us -> 0.01 us
  waiting for transfers between devices: 81.6 us -> 0 us
  Pallas kernels: 0 us -> 66.9 us
  matrix products: 26.9 us -> 0 us
  between operations: 14.2 us -> 0.02 us
    gather x4 -> x0, local copies, waits for them, and re-layouts: 194 us -> none  [row_terms(): return jnp.take(tile.reshape(-1), flat_index, axis=0)]
    pallas_call x0 -> x1, Pallas kernels: none -> 66.9 us  [shards(): pl.pallas_call(kernel, out_shape=jax.ShapeDtypeStruct((1, STOPS, PAIRS //...]
    ppermute x3 -> x0, waiting for transfers between devices: 54.5 us -> none  [from_behind(): return lax.ppermute(block, axis, route)]
    unnamed x17 -> x2, local copies, waits for them, and re-layouts: 33.7 us -> 0.01 us
    unnamed x2 -> x0, waiting for transfers between devices: 27.2 us -> none
    dot_general x4 -> x0, matrix products: 26.9 us -> none  [row_terms(): lax.dot_general(own_block, peer_block, (((1,), (1,)), ((), ())), preferre...]
  transfers between devices with their start and end apart: 4 -> 0, of which waited for: 3 -> 0; matrix products, arithmetic and copies ran while one was open for 54% -> 0% of each run, Pallas kernels for 0% -> 0%
where the time goes in v2:
time: 68.5 us; the launch traced here: 68.3 us
  Pallas kernels  66.9 us (98%)
  other arithmetic  1.45 us (2%)
    pallas_call x1, Pallas kernels, shards(): pl.pallas_call(kernel, out_shape=jax.ShapeDtypeStruct((1, STOPS, PAIRS //...  66.9 us
    select_n x1, other arithmetic, shards(): return jnp.where(live, sums / SNPS, jnp.zeros_like(sums))  1.45 us

profile of v2, /device:TPU:0, one launch (start us, length us, event | category | flops | bytes accessed | tf_op | source)
XLA Modules:
  0.0 68.3 jit_solution(1325469370579068587)
XLA Ops:
  0.0 0.0 copy-start
  0.0 66.9 %shard_map.49 = f32[1,4,2048]{2,1,0:T(4,128)} custom-call(bf16[2048,512]{1,0:T(8,128)(2,1)} %x.1, s32[1,4,4096]{2,1,0:T(4,128)} %row_hbm.1, s32[1,4,4096]{2,1,0:T(4,128)} %col_hbm.1), custom_call_target="tpu_custom_call" | custom-call | flops 17179869184 | bytes 4194304 | tf_op jit(solution)/shard_map/pallas_call | solution.py:334
  66.9 0.0 copy-done
  66.9 1.4 %multiply_select_fusion = f32[1,4,2048]{2,1,0:T(4,128)} fusion(f32[1,4,2048]{2,1,0:T(4,128)} %shard_map.49, s32[2048]{0:T(1024)S(1)} %iota_add_fusion, s32[4]{0:T(128)S(1)} %bitcast.1), kind=kLoop, calls=%fused_computation | loop fusion | flops 24576 | bytes 73744 | tf_op jit(solution)/shard_map/jit(_where)/select_n | solution.py:365
  (1 shorter events, 0.0 us)
Async XLA Ops:
  0.0 66.9 %copy-start = (s32[1,4]{1,0:T(1,128)S(1)}, s32[1,4]{1,0:T(1,128)}, u32[]{:S(2)}) copy-start(s32[1,4]{1,0:T(1,128)} %param.7) | copy-start | bytes 52

commit v3 on v2

--- a/solution.py
+++ b/solution.py
@@ -20,6 +20,7 @@
 SHARE = LIST // 2
 ROWS = LIST // CHUNKS
 STEPS = 5
+FIRST = 5
 UNROLL = 2
 
 OWN, LEFT, RIGHT, OTHER = 0, 1, 2, 3
@@ -84,7 +85,7 @@
         x.at[:, pl.ds(pl.multiple_of((1 - core) * QUARTER, QUARTER), QUARTER)], own_quart, list_sem.at[2])
     load_own.start()
     send_sib.start()
-    for n in range(CHUNKS):
+    for n in range(FIRST):
         send_main(n).start()
     load_row.start()
     load_col.start()
@@ -99,7 +100,10 @@
 
     def load_slots(step):
         return pltpu.make_async_copy(
-            addr_v.at[pl.ds(step * LIST, UNROLL * ROWS)], slots[step % 2], addr_sem.at[step % 2, 0])
+            addr_v.at[pl.ds(step * LIST, UNROLL * ROWS)], slots[step % 2].at[pl.ds(0, UNROLL * ROWS)], addr_sem.at[step % 2, 0])
+
+    def load_all_slots(step):
+        return pltpu.make_async_copy(addr_v.at[pl.ds(step * LIST, LIST)], slots[step % 2], addr_sem.at[step % 2, 0])
 
     def reload_slots(step, m, n):
         return pltpu.make_async_copy(
@@ -137,6 +141,8 @@
                 pair_v[s * LIST + k:s * LIST + k + 1, :] = pairs[s:s + 1, :]
         ask(0).start()
         ask(1).start()
+        for n in range(FIRST, CHUNKS):
+            send_main(n).start()
         prepare(0)
         load_slots(0).start()
         prepare(1)
@@ -208,7 +214,7 @@
                     if parts[step][2] is None:
                         land[0, parts[step][0]] = share(step, snp)[...]
 
-    for step in range(STEPS + 1):
+    for step in range(STEPS - 1):
         if step == 1:
             read_lists()
             send_sib.wait_recv()
@@ -221,12 +227,12 @@
                 send_main(n).wait_send()
             for n in range(CHUNKS // 2):
                 send_quarter(n).start()
-        if step == 4:
-            load_part.wait()
         if step > 0:
             load_slots(step - 1).wait()
-        if 0 < step < STEPS:
+        if 0 < step < 3:
             load_slots(step).start()
+        if step == 3:
+            load_all_slots(3).start()
 
         @pl.loop(0, CHUNKS // UNROLL)
         def _(m):
@@ -248,8 +254,6 @@
                     @pl.when(odd_core)
                     def _():
                         pass_on(n).wait_recv()
-                if step == 4:
-                    send_quarter(n).wait_recv()
                 if step > 0:
                     @pl.when(m > 0)
                     def _():
@@ -273,15 +277,13 @@
                     @pl.when(even_core)
                     def _():
                         multiply(step, n, 0)
-                elif 0 < step < STEPS:
+                elif step == 3:
                     @pl.when(core < 2)
                     def _():
                         multiply(step, n)
                         read_out(step - 1, n, q)
-                elif step == 0:
+                else:
                     multiply(step, n)
-                else:
-                    read_out(step - 1, n, q)
 
                 if step > 0:
                     @pl.when(m < CHUNKS // UNROLL - 1)
@@ -289,6 +291,24 @@
                         reload_slots(step - 1, m, q).start()
         if step > 0:
             hand_out(step - 1)
+
+    load_all_slots(4).start()
+    load_all_slots(3).wait()
+    for n in range(CHUNKS):
+        read_out(3, n, n)
+    hand_out(3)
+    load_part.wait()
+
+    @pl.loop(0, CHUNKS // UNROLL)
+    def _(m):
+        for q in range(UNROLL):
+            send_quarter(m * UNROLL + q).wait_recv()
+            multiply(4, m * UNROLL + q)
+
+    load_all_slots(4).wait()
+    for n in range(CHUNKS):
+        read_out(4, n, n)
+    hand_out(4)
 
     for n in range(CHUNKS):
         if n >= CHUNKS - 2:
@@ -347,8 +367,8 @@
             pltpu.VMEM((LISTS * LIST, 128), jnp.int32),
             pltpu.VMEM((STEPS * LIST, 128), jnp.int32),
             pltpu.VMEM((STEPS * LIST * 2, 128), jnp.int32),
-            pltpu.SMEM((UNROLL * ROWS, 128), jnp.int32),
-            pltpu.SMEM((UNROLL * ROWS, 128), jnp.int32),
+            pltpu.SMEM((LIST, 128), jnp.int32),
+            pltpu.SMEM((LIST, 128), jnp.int32),
             pltpu.VMEM((STEPS, LIST, 128), jnp.float32),
             pltpu.VMEM((4, STOPS, SHARE, 128), jnp.float32),
             dma, dma((3,)), dma((2, 1 + UNROLL)),

time: 68.5 us -> 62.7 us (0.915)
  Pallas kernels: 66.9 us -> 60.6 us
    pallas_call x1, Pallas kernels: 66.9 us -> 60.6 us  [shards(): pl.pallas_call(kernel, out_shape=jax.ShapeDtypeStruct((1, STOPS, PAIRS //...]
where the time goes in v3:
time: 62.7 us; the launch traced here: 62.1 us
  Pallas kernels  60.6 us (97%)
  other arithmetic  1.45 us (2%)
    pallas_call x1, Pallas kernels, shards(): pl.pallas_call(kernel, out_shape=jax.ShapeDtypeStruct((1, STOPS, PAIRS //...  60.6 us
    select_n x1, other arithmetic, shards(): return jnp.where(live, sums / SNPS, jnp.zeros_like(sums))  1.45 us

profile of v3, /device:TPU:0, one launch (start us, length us, event | category | flops | bytes accessed | tf_op | source)
XLA Modules:
  0.0 62.1 jit_solution(17930062897680026908)
XLA Ops:
  0.0 0.0 copy-start
  0.0 60.6 %shard_map.49 = f32[1,4,2048]{2,1,0:T(4,128)} custom-call(bf16[2048,512]{1,0:T(8,128)(2,1)} %x.1, s32[1,4,4096]{2,1,0:T(4,128)} %row_hbm.1, s32[1,4,4096]{2,1,0:T(4,128)} %col_hbm.1), custom_call_target="tpu_custom_call" | custom-call | flops 17179869184 | bytes 4194304 | tf_op jit(solution)/shard_map/pallas_call | solution.py:354
  60.6 0.0 copy-done
  60.6 1.4 %multiply_select_fusion = f32[1,4,2048]{2,1,0:T(4,128)} fusion(f32[1,4,2048]{2,1,0:T(4,128)} %shard_map.49, s32[2048]{0:T(1024)S(1)} %iota_add_fusion, s32[4]{0:T(128)S(1)} %bitcast.1), kind=kLoop, calls=%fused_computation | loop fusion | flops 24576 | bytes 73744 | tf_op jit(solution)/shard_map/jit(_where)/select_n | solution.py:385
  (1 shorter events, 0.0 us)
Async XLA Ops:
  0.0 60.6 %copy-start = (s32[1,4]{1,0:T(1,128)S(1)}, s32[1,4]{1,0:T(1,128)}, u32[]{:S(2)}) copy-start(s32[1,4]{1,0:T(1,128)} %param.7) | copy-start | bytes 52

commit v4 on v3

--- a/solution.py
+++ b/solution.py
@@ -223,10 +223,6 @@
             ask(1).wait_recv()
             for later in range(2, STEPS):
                 prepare(later)
-            for n in range(CHUNKS - 2):
-                send_main(n).wait_send()
-            for n in range(CHUNKS // 2):
-                send_quarter(n).start()
         if step > 0:
             load_slots(step - 1).wait()
         if 0 < step < 3:
@@ -248,7 +244,9 @@
                     if q == 0:
                         @pl.when(n == CHUNKS - UNROLL)
                         def _():
-                            for i in range(CHUNKS // 2, CHUNKS):
+                            for i in range(CHUNKS):
+                                send_main(i).wait_send()
+                            for i in range(CHUNKS):
                                 send_quarter(i).start()
                 if step == 3:
                     @pl.when(odd_core)
@@ -311,8 +309,6 @@
     hand_out(4)
 
     for n in range(CHUNKS):
-        if n >= CHUNKS - 2:
-            send_main(n).wait_send()
         send_quarter(n).wait_send()
     send_sib.wait_send()
     ask(0).wait_send()

time: 62.7 us -> 61.5 us (0.981)
  the two profiles are of different devices: /device:TPU:0 before, /device:TPU:1 now
where the time goes in v4:
time: 61.5 us; the launch traced here: 61.3 us
  Pallas kernels  59.8 us (97%)
  other arithmetic  1.45 us (2%)
    pallas_call x1, Pallas kernels, shards(): pl.pallas_call(kernel, out_shape=jax.ShapeDtypeStruct((1, STOPS, PAIRS //...  59.8 us
    select_n x1, other arithmetic, shards(): return jnp.where(live, sums / SNPS, jnp.zeros_like(sums))  1.45 us

profile of v4, /device:TPU:1, one launch (start us, length us, event | category | flops | bytes accessed | tf_op | source)
XLA Modules:
  0.0 61.3 jit_solution(4685893646647953891)
XLA Ops:
  0.0 0.0 copy-start
  0.0 59.8 %shard_map.49 = f32[1,4,2048]{2,1,0:T(4,128)} custom-call(bf16[2048,512]{1,0:T(8,128)(2,1)} %x.1, s32[1,4,4096]{2,1,0:T(4,128)} %row_hbm.1, s32[1,4,4096]{2,1,0:T(4,128)} %col_hbm.1), custom_call_target="tpu_custom_call" | custom-call | flops 17179869184 | bytes 4194304 | tf_op jit(solution)/shard_map/pallas_call | solution.py:350
  59.9 0.0 copy-done
  59.9 1.4 %multiply_select_fusion = f32[1,4,2048]{2,1,0:T(4,128)} fusion(f32[1,4,2048]{2,1,0:T(4,128)} %shard_map.49, s32[2048]{0:T(1024)S(1)} %iota_add_fusion, s32[4]{0:T(128)S(1)} %bitcast.1), kind=kLoop, calls=%fused_computation | loop fusion | flops 24576 | bytes 73744 | tf_op jit(solution)/shard_map/jit(_where)/select_n | solution.py:381
  (1 shorter events, 0.0 us)
Async XLA Ops:
  0.0 59.9 %copy-start = (s32[1,4]{1,0:T(1,128)S(1)}, s32[1,4]{1,0:T(1,128)}, u32[]{:S(2)}) copy-start(s32[1,4]{1,0:T(1,128)} %param.7) | copy-start | bytes 52
